TPU v7x, 32 devices: a whole 2x2x4 slice. The times are simulated.
32 devices in a mesh: island: 4 (over y, x), fsdp: 8 (over z, core).
Axes of the slice: x: 2, y: 2, z: 4, core: 2. Of those that a mesh axis runs over, the one named last changes fastest.
Arguments:
- global_params: bfloat16 [4, 1, 4096, 8192], P('island', None, 'fsdp'), may hold values from -6 to 6
- local_params: bfloat16 [4, 1, 4096, 8192], P('island', None, 'fsdp'), may hold values from -6 to 6
- momentum: bfloat16 [4, 1, 4096, 8192], P('island', None, 'fsdp'), may hold values from -6 to 6
- init_factors: float32 [4, 1, 4, 8192], replicated, may hold values from -6 to 6
- seeds: int32 [4], replicated, may hold values from 0 to 3, as said below
- plan: int32 [8], replicated, may hold values from 1 to 2, as said below
- round_index: int32 [], replicated, may hold values from 0 to 999
Outputs:
- new_params: bfloat16 [4, 1, 4096, 8192], P('island', None, 'fsdp')
- new_momentum: bfloat16 [4, 1, 4096, 8192], P('island', None, 'fsdp')
- warm_factors: float32 [4, 1, 4, 8192], P('island')
Inputs may be any that keep to these rules, and one draw needn't show every extreme that they name: `plan`: every entry is a power of two; every power of two up to 2 appears. `seeds`: every value from 0 to 3 is used by some replica.
All inputs are finite; a program needn't handle non-finite values.
Results may differ from a plain program's by a relative error of at most 0.0017.
Values sent between devices are 32-bit elements; how exact they have to be, the bound alone decides.
A program may use at most 128 MiB of HBM per device.

v0:
```python
import functools

import jax
import jax.numpy as jnp
from jax import lax
from jax.experimental import pallas as pl
from jax.experimental.pallas import tpu as pltpu
from jax.sharding import PartitionSpec as P

ITERS = 3
MESH = pl.DeviceIdType.MESH
F32, BF16 = jnp.float32, jnp.bfloat16
NT = (((1,), (1,)), ((), ()))
NN = (((1,), (0,)), ((), ()))


def dot(a, b, dims):
    return lax.dot_general(a, b, dims, preferred_element_type=F32)


def rounded(x):
    return x.astype(BF16).astype(F32)


def three_parts(x):
    high = rounded(x)
    rest = x - high
    middle = rounded(rest)
    return jnp.concatenate([high, middle, rest - middle, jnp.zeros_like(x)], axis=0).astype(BF16)


def folded(x, rank):
    return x[0:rank] + x[rank : 2 * rank] + x[2 * rank : 3 * rank]


def cholesky(gram, rank):
    lower, inverse = {}, {}
    for j in range(rank):
        square = gram[j : j + 1, j : j + 1]
        for k in range(j):
            square = square - lower[j, k] * lower[j, k]
        inverse[j] = 1.0 / jnp.sqrt(square)
        for i in range(j + 1, rank):
            entry = gram[i : i + 1, j : j + 1]
            for k in range(j):
                entry = entry - lower[i, k] * lower[j, k]
            lower[i, j] = entry * inverse[j]
    return lower, inverse


def solved(factors, x):
    lower, inverse = factors
    rows = []
    for i in range(x.shape[0]):
        row = x[i : i + 1]
        for k in range(i):
            row = row - lower[i, k] * rows[k]
        rows.append(row * inverse[i])
    return jnp.concatenate(rows, axis=0)


def gossip_kernel(
    level, shards, g_hbm, l_hbm, q_ref, warm_ref, fac_ref, bas_ref,
    hi, lo, g_buf, l_buf, qs, acc, p_out, p_in, rs_out, rs_in, gathered, grams,
    load_sem, p_sem, rs_send, rs_recv, ag_send, ag_recv, gram_send, gram_recv,
):
    rank, cols = q_ref.shape
    rows = hi.shape[0]
    members = 2 * shards
    width = cols // members
    island, shard = lax.axis_index("island"), lax.axis_index("fsdp")
    step = 1 << level
    side = lax.rem(lax.div(island, step), 2)
    me = side * shards + shard

    def device(k):
        return (island + (lax.div(k, shards) - side) * step, lax.rem(k, shards))

    def block(k):
        return pl.ds(pl.multiple_of(k * width, width), width)

    def after(k):
        return lax.rem(me + k, members)

    barrier = pltpu.get_barrier_semaphore()

    @pl.loop(1, members)
    def _(k):
        pl.semaphore_signal(barrier, inc=1, device_id=device(after(k)), device_id_type=MESH)

    part = g_buf.shape[1]
    parts = rows // part

    def load(i, slot):
        at = pl.ds(pl.multiple_of(i * part, part), part)
        return (
            pltpu.make_async_copy(g_hbm.at[at], g_buf.at[slot], load_sem.at[0, slot]),
            pltpu.make_async_copy(l_hbm.at[at], l_buf.at[slot], load_sem.at[1, slot]),
        )

    for copy in load(0, 0):
        copy.start()
    qs[...] = three_parts(q_ref[...])
    acc[...] = jnp.zeros_like(acc)
    piece = min(512, cols)

    @pl.loop(0, parts)
    def _(i):
        slot = lax.rem(i, 2)

        @pl.when(i + 1 < parts)
        def _():
            for copy in load(i + 1, 1 - slot):
                copy.start()

        for copy in load(i, slot):
            copy.wait()
        at = pl.ds(pl.multiple_of(i * part, part), part)
        total = jnp.zeros((part, 4 * rank), F32)
        for c in range(0, cols, piece):
            delta = g_buf[slot, :, c : c + piece].astype(F32) - l_buf[slot, :, c : c + piece].astype(F32)
            high = delta.astype(BF16)
            low = (delta - high.astype(F32)).astype(BF16)
            hi[at, c : c + piece] = high
            lo[at, c : c + piece] = low
            factor = qs[:, c : c + piece]
            total = total + dot(high, factor, NT) + dot(low, factor, NT)
        acc[at, 0 : 4 * rank] = total

    pl.semaphore_wait(barrier, members - 1)

    factors = None
    for turn in range(ITERS):
        product = folded(acc[...].T, rank)
        if turn:
            product = solved(factors, product)
        p_out[...] = product
        swap = pltpu.make_async_remote_copy(
            src_ref=p_out, dst_ref=p_in, send_sem=p_sem.at[0], recv_sem=p_sem.at[1],
            device_id=(island + (1 - 2 * side) * step, shard), device_id_type=MESH,
        )
        swap.start()
        swap.wait()
        left = product - p_in[...]

        lane = lax.broadcasted_iota(jnp.int32, (rank, 128), 1)
        gram = jnp.zeros((rank, 128), F32)
        for j in range(rank):
            column = jnp.sum(left * left[j : j + 1], axis=1, keepdims=True)
            gram = jnp.where(lane == j, column, gram)
        grams[turn, pl.ds(shard, 1)] = gram[None]

        def gram_copy(k):
            to = lax.rem(shard + k, shards)
            return pltpu.make_async_remote_copy(
                src_ref=grams.at[turn, shard], dst_ref=grams.at[turn, shard],
                send_sem=gram_send.at[turn, to], recv_sem=gram_recv.at[turn, shard],
                device_id=(island, to), device_id_type=MESH,
            )

        def gram_arrival(k):
            at = lax.rem(shard + k, shards)
            return pltpu.make_async_remote_copy(
                src_ref=grams.at[turn, at], dst_ref=grams.at[turn, at],
                send_sem=gram_send.at[turn, at], recv_sem=gram_recv.at[turn, at],
                device_id=(island, at), device_id_type=MESH,
            )

        @pl.loop(1, shards)
        def _(k):
            gram_copy(k).start()

        left_parts = three_parts(left)

        def raw(b):
            at = block(b)
            return folded(dot(left_parts, hi[:, at], NN) + dot(left_parts, lo[:, at], NN), rank)

        def scatter(b):
            return pltpu.make_async_remote_copy(
                src_ref=rs_out.at[b], dst_ref=rs_in.at[me],
                send_sem=rs_send.at[b], recv_sem=rs_recv.at[me],
                device_id=device(b), device_id_type=MESH,
            )

        def scatter_arrival(k):
            return pltpu.make_async_remote_copy(
                src_ref=rs_out.at[k], dst_ref=rs_in.at[k],
                send_sem=rs_send.at[k], recv_sem=rs_recv.at[k],
                device_id=device(k), device_id_type=MESH,
            )

        @pl.loop(1, members)
        def _(k):
            b = after(k)
            rs_out[pl.ds(b, 1)] = raw(b)[None]
            scatter(b).start()

        rs_in[pl.ds(me, 1)] = raw(me)[None]

        @pl.loop(1, members)
        def _(k):
            scatter_arrival(after(members - k)).wait_recv()

        gathered[pl.ds(me, 1)] = jnp.sum(rs_in[...], axis=0, keepdims=True)

        def gather(b):
            return pltpu.make_async_remote_copy(
                src_ref=gathered.at[me], dst_ref=gathered.at[me],
                send_sem=ag_send.at[b], recv_sem=ag_recv.at[me],
                device_id=device(b), device_id_type=MESH,
            )

        def gather_arrival(k):
            return pltpu.make_async_remote_copy(
                src_ref=gathered.at[k], dst_ref=gathered.at[k],
                send_sem=ag_send.at[k], recv_sem=ag_recv.at[k],
                device_id=device(k), device_id_type=MESH,
            )

        @pl.loop(1, members)
        def _(k):
            gather(after(k)).start()

        def normaliser():
            @pl.loop(1, shards)
            def _(k):
                gram_arrival(k).wait_recv()

            return cholesky(jnp.sum(grams[turn], axis=0), rank)

        if turn < ITERS - 1:

            def right(b):
                at = block(b)
                factor = three_parts(gathered[b])
                return dot(hi[:, at], factor, NT) + dot(lo[:, at], factor, NT)

            acc[:, 0 : 4 * rank] = right(me)

            @pl.loop(1, members)
            def _(k):
                b = after(members - k)
                gather_arrival(b).wait_recv()
                acc[:, 0 : 4 * rank] += right(b)

            factors = normaliser()
        else:
            factors = normaliser()
            basis = 0.5 * solved(factors, left)
            high = rounded(basis)
            stack = jnp.concatenate([high, high, basis - high, jnp.zeros_like(basis)], axis=0)
            bas_ref[...] = jnp.concatenate([stack, jnp.zeros((128 - 4 * rank, rows), F32)], axis=0).T.astype(BF16)

            def finish(b):
                at = block(b)
                factor = solved(factors, gathered[b])
                warm_ref[:, at] = factor
                high = rounded(factor)
                fac_ref[:, at] = jnp.concatenate([high, factor - high, high, jnp.zeros_like(high)], axis=0).astype(BF16)

            finish(me)

            @pl.loop(1, members)
            def _(k):
                b = after(members - k)
                gather_arrival(b).wait_recv()
                finish(b)

        @pl.loop(1, members)
        def _(k):
            b = after(k)
            scatter(b).wait_send()
            gather(b).wait_send()

        @pl.loop(1, shards)
        def _(k):
            gram_copy(k).wait_send()


def gossip(level, shards, g, l, q):
    rows, cols = g.shape
    rank = q.shape[0]
    members = 2 * shards
    width = cols // members
    part = min(64, rows)
    vmem = pl.BlockSpec(memory_space=pltpu.VMEM)
    hbm = pl.BlockSpec(memory_space=pl.ANY)
    dma = pltpu.SemaphoreType.DMA
    return pl.pallas_call(
        functools.partial(gossip_kernel, level, shards),
        out_shape=(
            jax.ShapeDtypeStruct((rank, cols), F32),
            jax.ShapeDtypeStruct((4 * rank, cols), BF16),
            jax.ShapeDtypeStruct((rows, 128), BF16),
        ),
        in_specs=[hbm, hbm, vmem],
        out_specs=(vmem, vmem, vmem),
        scratch_shapes=[
            pltpu.VMEM((rows, cols), BF16),
            pltpu.VMEM((rows, cols), BF16),
            pltpu.VMEM((2, part, cols), BF16),
            pltpu.VMEM((2, part, cols), BF16),
            pltpu.VMEM((4 * rank, cols), BF16),
            pltpu.VMEM((rows, 128), F32),
            pltpu.VMEM((rank, rows), F32),
            pltpu.VMEM((rank, rows), F32),
            pltpu.VMEM((members, rank, width), F32),
            pltpu.VMEM((members, rank, width), F32),
            pltpu.VMEM((members, rank, width), F32),
            pltpu.VMEM((ITERS, shards, rank, 128), F32),
            dma((2, 2)),
            dma((2,)),
            dma((members,)),
            dma((members,)),
            dma((members,)),
            dma((members,)),
            dma((ITERS, shards)),
            dma((ITERS, shards)),
        ],
        compiler_params=pltpu.CompilerParams(
            collective_id=level + 1, has_side_effects=True, vmem_limit_bytes=44 << 20
        ),
        cost_estimate=pl.CostEstimate(
            flops=12 * ITERS * rank * rows * cols, bytes_accessed=4 * rows * cols, transcendentals=0
        ),
    )(g, l, q)


def outer_kernel(bas_ref, fac_ref, g_ref, l_ref, m_ref, params_ref, momentum_ref):
    depth, cols = fac_ref.shape
    basis = bas_ref[:, 0:depth]
    piece = min(1024, cols)
    for c in range(0, cols, piece):
        at = slice(c, c + piece)
        start = g_ref[:, at].astype(F32)
        gossiped = start - l_ref[:, at].astype(F32) - dot(basis, fac_ref[:, at], NN)
        velocity = 0.9 * m_ref[:, at].astype(F32) + gossiped
        params_ref[:, at] = (start - 0.7 * (gossiped + 0.9 * velocity)).astype(BF16)
        momentum_ref[:, at] = velocity.astype(BF16)


def outer_step(bas, fac, g, l, m):
    rows, cols = g.shape
    part = min(32, rows)
    wide = pl.BlockSpec((part, cols), lambda i: (i, 0))
    return pl.pallas_call(
        outer_kernel,
        grid=(rows // part,),
        out_shape=(jax.ShapeDtypeStruct((rows, cols), BF16),) * 2,
        in_specs=[
            pl.BlockSpec((part, bas.shape[1]), lambda i: (i, 0)),
            pl.BlockSpec(fac.shape, lambda i: (0, 0)),
            wide, wide, wide,
        ],
        out_specs=(wide, wide),
        compiler_params=pltpu.CompilerParams(vmem_limit_bytes=24 << 20),
        cost_estimate=pl.CostEstimate(
            flops=2 * fac.shape[0] * rows * cols, bytes_accessed=10 * rows * cols, transcendentals=0
        ),
    )(bas, fac, g, l, m)


def on_device(global_params, local_params, momentum, init_factors, seeds, plan, round_index):
    shape = global_params.shape
    g, l, m = (x.reshape(shape[-2:]) for x in (global_params, local_params, momentum))
    offset = plan[jnp.mod(round_index, plan.shape[0])]
    island = lax.axis_index("island")
    factor = init_factors[seeds[jnp.minimum(island, jnp.bitwise_xor(island, offset))], 0]
    levels = lax.axis_size("island").bit_length() - 1
    shards = lax.axis_size("fsdp")
    level_ids = jnp.arange(levels, dtype=jnp.int32)
    which_bit = jnp.sum(jnp.where(jnp.left_shift(jnp.int32(1), level_ids) == offset, level_ids, 0))
    branches = [functools.partial(gossip, level, shards) for level in range(levels)]
    warm, fac, bas = lax.switch(which_bit, branches, g, l, factor)
    params, velocity = outer_step(bas, fac, g, l, m)
    return params.reshape(shape), velocity.reshape(shape), warm[None, None]


def solution(mesh):
    return jax.shard_map(
        on_device,
        mesh=mesh,
        in_specs=(
            P("island", None, "fsdp", None),
            P("island", None, "fsdp", None),
            P("island", None, "fsdp", None),
            P(),
            P(),
            P(),
            P(),
        ),
        out_specs=(
            P("island", None, "fsdp", None),
            P("island", None, "fsdp", None),
            P("island", None, None, None),
        ),
        check_vma=False,
    )
```

profile of v0, /device:TPU:0, one launch (start us, length us, event | category | flops | bytes accessed | tf_op | source)
XLA Modules:
  0.0 104.8 jit_solution(13113889426061733436)
XLA Ops:
  1.3 1.2 %dynamic_slice.19 = s32[1]{0:T(128)} dynamic-slice(s32[8]{0:T(128)} %param.14, s32[]{:T(128)S(6)} %select_n.27), dynamic_slice_sizes={1} | dynamic-slice | bytes 12 | tf_op jit(solution)/shard_map/dynamic_slice | solution.py:367
  3.2 1.3 %fusion = s32[]{:T(128)} fusion(s32[]{:T(128)} %bitcast.4), kind=kLoop, calls=%fused_computation.3 | loop fusion | flops 7 | bytes 8 | tf_op jit(solution)/shard_map/reduce_sum | solution.py:373
  5.1 1.2 %dynamic_slice.20 = s32[1]{0:T(128)} dynamic-slice(s32[4]{0:T(128)} %param.13, s32[]{:T(128)S(6)} %select_n.29), dynamic_slice_sizes={1} | dynamic-slice | bytes 12 | tf_op jit(solution)/shard_map/dynamic_slice | solution.py:369
  6.4 73.9 %conditional.1 = (bf16[16,8192]{1,0:T(8,128)(2,1)S(1)}, bf16[512,128]{1,0:T(8,128)(2,1)S(1)}, f32[1,1,4,8192]{3,2,1,0:T(4,128)S(1)}) conditional(s32[]{:T(128)} %clamp.3, (s32[]{:T(128)}, f32[4,1,4,8192]{3,2,1,0:T(4,128)}, bf16[512,8192]{1,0:T(8,128)(2,1)}, bf16[512,8192]{1,0:T(8,128)(2,1)}) %tuple.30, (s32[]{:T(128)}, f32[4,1,4,8192]{3,2,1,0:T(4,128)}, ...), branch_computations={%region_1.2_spmd, %region_2.3_spmd} | conditional | flops 603979776 | bytes 17039422 | solution.py:375
  8.3 0.9 dynamic-slice_bitcast_fusion.1.q_ref
  9.2 71.0 %branch_1_fun.2 = (f32[4,8192]{1,0:T(4,128)S(1)}, bf16[16,8192]{1,0:T(8,128)(2,1)S(1)}, bf16[512,128]{1,0:T(8,128)(2,1)S(1)}) custom-call(bf16[512,8192]{1,0:T(8,128)(2,1)} %get-tuple-element.86.g_hbm, bf16[512,8192]{1,0:T(8,128)(2,1)} %get-tuple-element.87.l_hbm, f32[4,8192]{1,0:T(4,128)S(1)} %dynamic-slice_bitcast_fusion.1.q_ref), custom_call_target="tpu_custom_call" | custom-call | flops 603979776 | bytes 16777216 | tf_op jit(solution)/shard_map/cond/branch_1_fun/pallas_call | solution.py:290
  80.2 0.0 copy-start
  80.3 3.4 %copy-done = bf16[1,1,512,8192]{3,2,1,0:T(8,128)(2,1)S(1)} copy-done((bf16[1,1,512,8192]{3,2,1,0:T(8,128)(2,1)S(1)}, bf16[1,1,512,8192]{3,2,1,0:T(8,128)(2,1)}, u32[]{:S(2)}) %copy-start) | copy-done | bytes 8388632
  83.6 20.5 %shard_map.94 = (bf16[512,8192]{1,0:T(8,128)(2,1)}, bf16[512,8192]{1,0:T(8,128)(2,1)}) custom-call(bf16[512,128]{1,0:T(8,128)(2,1)S(1)} %get-tuple-element.101.bas_ref, bf16[16,8192]{1,0:T(8,128)(2,1)S(1)} %get-tuple-element.102.fac_ref, bf16[512,8192]{1,0:T(8,128)(2,1)} %bitcast.16, bf16[512,8192]{1,0:T(8,128)(2,1)} %bitcast.19, bf16[512,8192]{1,0:T(8,128)(2,1)S(1)} %bitcast.13), custom_call_target="tpu_custom_call" | custom-call | flops 134217728 | bytes 41943040 | tf_op jit(solution)/shard_map/pallas_call | solution.py:347
  104.1 0.7 copy.18
Async XLA Ops:
  80.2 3.4 %copy-start = (bf16[1,1,512,8192]{3,2,1,0:T(8,128)(2,1)S(1)}, bf16[1,1,512,8192]{3,2,1,0:T(8,128)(2,1)}, u32[]{:S(2)}) copy-start(bf16[1,1,512,8192]{3,2,1,0:T(8,128)(2,1)} %param.11) | copy-start | bytes 25165828
where the time goes:
time: 106 us; the launch traced here: 105 us
  Pallas kernels  91.5 us (86%)
  local copies, waits for them, and re-layouts  7.43 us (7%)
  between operations  2.63 us (2%)
  loops' own time  1.95 us (2%)
  other arithmetic  1.28 us (1%)
    pallas_call x1, Pallas kernels, gossip(): pl.pallas_call(functools.partial(gossip_kernel, level, shards), out_shape...  71 us
    pallas_call x1, Pallas kernels, outer_step(): pl.pallas_call(outer_kernel, grid=(rows // part,), out_shape=(jax.ShapeDt...  20.5 us
    unnamed x3, local copies, waits for them, and re-layouts  4.03 us

commit v1 on v0

--- a/solution.py
+++ b/solution.py
@@ -60,14 +60,16 @@
 
 
 def gossip_kernel(
-    level, shards, g_hbm, l_hbm, q_ref, warm_ref, fac_ref, bas_ref,
-    hi, lo, g_buf, l_buf, qs, acc, p_out, p_in, rs_out, rs_in, gathered, grams,
+    level, shards, seeds_ref, g_hbm, l_hbm, init_ref, warm_ref, fac_ref, bas_ref,
+    hi, lo, g_buf, l_buf, acc, p_out, p_in, rs_out, rs_in, gathered, grams,
     load_sem, p_sem, rs_send, rs_recv, ag_send, ag_recv, gram_send, gram_recv,
 ):
-    rank, cols = q_ref.shape
+    rank, cols = init_ref.shape[1:]
     rows = hi.shape[0]
     members = 2 * shards
     width = cols // members
+    bundle = 4 if members % 4 == 0 else 1
+    bundles = members // bundle
     island, shard = lax.axis_index("island"), lax.axis_index("fsdp")
     step = 1 << level
     side = lax.rem(lax.div(island, step), 2)
@@ -79,6 +81,19 @@
     def block(k):
         return pl.ds(pl.multiple_of(k * width, width), width)
 
+    def columns(k):
+        return pl.ds(pl.multiple_of(k * (bundle * width), bundle * width), bundle * width)
+
+    mine = lax.div(me, bundle)
+
+    def others(k, act):
+        for j in range(bundle):
+            b = k * bundle + j
+
+            @pl.when(b != me)
+            def _():
+                act(b)
+
     def after(k):
         return lax.rem(me + k, members)
 
@@ -88,21 +103,25 @@
     def _(k):
         pl.semaphore_signal(barrier, inc=1, device_id=device(after(k)), device_id_type=MESH)
 
-    part = g_buf.shape[1]
-    parts = rows // part
+    part = g_buf.shape[2]
+    parts = cols // part
+    tall = min(32, rows)
 
     def load(i, slot):
         at = pl.ds(pl.multiple_of(i * part, part), part)
         return (
-            pltpu.make_async_copy(g_hbm.at[at], g_buf.at[slot], load_sem.at[0, slot]),
-            pltpu.make_async_copy(l_hbm.at[at], l_buf.at[slot], load_sem.at[1, slot]),
+            pltpu.make_async_copy(g_hbm.at[:, at], g_buf.at[slot], load_sem.at[0, slot]),
+            pltpu.make_async_copy(l_hbm.at[:, at], l_buf.at[slot], load_sem.at[1, slot]),
         )
 
     for copy in load(0, 0):
         copy.start()
-    qs[...] = three_parts(q_ref[...])
+    seed = seeds_ref[jnp.minimum(island, island + (1 - 2 * side) * step)]
     acc[...] = jnp.zeros_like(acc)
-    piece = min(512, cols)
+
+    def right(at, factor):
+        parts = three_parts(factor)
+        return dot(hi[:, at], parts, NT) + dot(lo[:, at], parts, NT)
 
     @pl.loop(0, parts)
     def _(i):
@@ -116,16 +135,12 @@
         for copy in load(i, slot):
             copy.wait()
         at = pl.ds(pl.multiple_of(i * part, part), part)
-        total = jnp.zeros((part, 4 * rank), F32)
-        for c in range(0, cols, piece):
-            delta = g_buf[slot, :, c : c + piece].astype(F32) - l_buf[slot, :, c : c + piece].astype(F32)
+        for r in range(0, rows, tall):
+            delta = g_buf[slot, r : r + tall].astype(F32) - l_buf[slot, r : r + tall].astype(F32)
             high = delta.astype(BF16)
-            low = (delta - high.astype(F32)).astype(BF16)
-            hi[at, c : c + piece] = high
-            lo[at, c : c + piece] = low
-            factor = qs[:, c : c + piece]
-            total = total + dot(high, factor, NT) + dot(low, factor, NT)
-        acc[at, 0 : 4 * rank] = total
+            hi[r : r + tall, at] = high
+            lo[r : r + tall, at] = (delta - high.astype(F32)).astype(BF16)
+        acc[:, 0 : 4 * rank] += right(at, init_ref[seed, :, at])
 
     pl.semaphore_wait(barrier, members - 1)
 
@@ -172,10 +187,6 @@
 
         left_parts = three_parts(left)
 
-        def raw(b):
-            at = block(b)
-            return folded(dot(left_parts, hi[:, at], NN) + dot(left_parts, lo[:, at], NN), rank)
-
         def scatter(b):
             return pltpu.make_async_remote_copy(
                 src_ref=rs_out.at[b], dst_ref=rs_in.at[me],
@@ -190,13 +201,16 @@
                 device_id=device(k), device_id_type=MESH,
             )
 
-        @pl.loop(1, members)
-        def _(k):
-            b = after(k)
-            rs_out[pl.ds(b, 1)] = raw(b)[None]
-            scatter(b).start()
-
-        rs_in[pl.ds(me, 1)] = raw(me)[None]
+        @pl.loop(1, bundles + 1)
+        def _(s):
+            k = lax.rem(mine + s, bundles)
+            at = columns(k)
+            raw = folded(dot(left_parts, hi[:, at], NN) + dot(left_parts, lo[:, at], NN), rank)
+            for j in range(bundle):
+                rs_out[pl.ds(k * bundle + j, 1)] = raw[None, :, j * width : (j + 1) * width]
+            others(k, lambda b: scatter(b).start())
+
+        rs_in[pl.ds(me, 1)] = rs_out[pl.ds(me, 1)]
 
         @pl.loop(1, members)
         def _(k):
@@ -218,9 +232,9 @@
                 device_id=device(k), device_id_type=MESH,
             )
 
-        @pl.loop(1, members)
-        def _(k):
-            gather(after(k)).start()
+        @pl.loop(0, bundles)
+        def _(s):
+            others(lax.rem(mine + s, bundles), lambda b: gather(b).start())
 
         def normaliser():
             @pl.loop(1, shards)
@@ -231,18 +245,20 @@
 
         if turn < ITERS - 1:
 
-            def right(b):
-                at = block(b)
-                factor = three_parts(gathered[b])
-                return dot(hi[:, at], factor, NT) + dot(lo[:, at], factor, NT)
-
-            acc[:, 0 : 4 * rank] = right(me)
-
-            @pl.loop(1, members)
-            def _(k):
-                b = after(members - k)
-                gather_arrival(b).wait_recv()
-                acc[:, 0 : 4 * rank] += right(b)
+            @pl.loop(0, bundles)
+            def _(s):
+                k = lax.rem(mine + bundles - s, bundles)
+                others(k, lambda b: gather_arrival(b).wait_recv())
+                factor = jnp.concatenate([gathered[k * bundle + j] for j in range(bundle)], axis=1)
+                total = right(columns(k), factor)
+
+                @pl.when(s == 0)
+                def _():
+                    acc[:, 0 : 4 * rank] = total
+
+                @pl.when(s > 0)
+                def _():
+                    acc[:, 0 : 4 * rank] += total
 
             factors = normaliser()
         else:
@@ -259,13 +275,12 @@
                 high = rounded(factor)
                 fac_ref[:, at] = jnp.concatenate([high, factor - high, high, jnp.zeros_like(high)], axis=0).astype(BF16)
 
-            finish(me)
-
-            @pl.loop(1, members)
-            def _(k):
-                b = after(members - k)
-                gather_arrival(b).wait_recv()
-                finish(b)
+            @pl.loop(0, bundles)
+            def _(s):
+                k = lax.rem(mine + bundles - s, bundles)
+                others(k, lambda b: gather_arrival(b).wait_recv())
+                for j in range(bundle):
+                    finish(k * bundle + j)
 
         @pl.loop(1, members)
         def _(k):
@@ -278,12 +293,12 @@
             gram_copy(k).wait_send()
 
 
-def gossip(level, shards, g, l, q):
+def gossip(level, shards, seeds, g, l, init):
     rows, cols = g.shape
-    rank = q.shape[0]
+    rank = init.shape[1]
     members = 2 * shards
     width = cols // members
-    part = min(64, rows)
+    part = min(1024, cols)
     vmem = pl.BlockSpec(memory_space=pltpu.VMEM)
     hbm = pl.BlockSpec(memory_space=pl.ANY)
     dma = pltpu.SemaphoreType.DMA
@@ -294,14 +309,13 @@
             jax.ShapeDtypeStruct((4 * rank, cols), BF16),
             jax.ShapeDtypeStruct((rows, 128), BF16),
         ),
-        in_specs=[hbm, hbm, vmem],
+        in_specs=[pl.BlockSpec(memory_space=pltpu.SMEM), hbm, hbm, vmem],
         out_specs=(vmem, vmem, vmem),
         scratch_shapes=[
             pltpu.VMEM((rows, cols), BF16),
             pltpu.VMEM((rows, cols), BF16),
-            pltpu.VMEM((2, part, cols), BF16),
-            pltpu.VMEM((2, part, cols), BF16),
-            pltpu.VMEM((4 * rank, cols), BF16),
+            pltpu.VMEM((2, rows, part), BF16),
+            pltpu.VMEM((2, rows, part), BF16),
             pltpu.VMEM((rows, 128), F32),
             pltpu.VMEM((rank, rows), F32),
             pltpu.VMEM((rank, rows), F32),
@@ -319,42 +333,44 @@
             dma((ITERS, shards)),
         ],
         compiler_params=pltpu.CompilerParams(
-            collective_id=level + 1, has_side_effects=True, vmem_limit_bytes=44 << 20
+            collective_id=level + 1, has_side_effects=True, vmem_limit_bytes=30 << 20
         ),
         cost_estimate=pl.CostEstimate(
             flops=12 * ITERS * rank * rows * cols, bytes_accessed=4 * rows * cols, transcendentals=0
         ),
-    )(g, l, q)
-
-
-def outer_kernel(bas_ref, fac_ref, g_ref, l_ref, m_ref, params_ref, momentum_ref):
-    depth, cols = fac_ref.shape
-    basis = bas_ref[:, 0:depth]
-    piece = min(1024, cols)
-    for c in range(0, cols, piece):
-        at = slice(c, c + piece)
-        start = g_ref[:, at].astype(F32)
-        gossiped = start - l_ref[:, at].astype(F32) - dot(basis, fac_ref[:, at], NN)
-        velocity = 0.9 * m_ref[:, at].astype(F32) + gossiped
-        params_ref[:, at] = (start - 0.7 * (gossiped + 0.9 * velocity)).astype(BF16)
-        momentum_ref[:, at] = velocity.astype(BF16)
+    )(seeds, g, l, init)
+
+
+def outer_kernel(bas_ref, fac_ref, g_ref, l_ref, m_ref, params_ref, momentum_ref, correction):
+    depth = fac_ref.shape[0]
+    rows = g_ref.shape[0]
+    correction[...] = dot(bas_ref[:, 0:depth], fac_ref[...], NN)
+    tall = min(32, rows)
+    for r in range(0, rows, tall):
+        at = slice(r, r + tall)
+        start = g_ref[at].astype(F32)
+        gossiped = start - l_ref[at].astype(F32) - correction[at]
+        velocity = 0.9 * m_ref[at].astype(F32) + gossiped
+        params_ref[at] = (start - 0.7 * (gossiped + 0.9 * velocity)).astype(BF16)
+        momentum_ref[at] = velocity.astype(BF16)
 
 
 def outer_step(bas, fac, g, l, m):
     rows, cols = g.shape
-    part = min(32, rows)
-    wide = pl.BlockSpec((part, cols), lambda i: (i, 0))
+    part = min(512, cols)
+    tile = pl.BlockSpec((rows, part), lambda i: (0, i))
     return pl.pallas_call(
         outer_kernel,
-        grid=(rows // part,),
+        grid=(cols // part,),
         out_shape=(jax.ShapeDtypeStruct((rows, cols), BF16),) * 2,
         in_specs=[
-            pl.BlockSpec((part, bas.shape[1]), lambda i: (i, 0)),
-            pl.BlockSpec(fac.shape, lambda i: (0, 0)),
-            wide, wide, wide,
+            pl.BlockSpec(bas.shape, lambda i: (0, 0)),
+            pl.BlockSpec((fac.shape[0], part), lambda i: (0, i)),
+            tile, tile, tile,
         ],
-        out_specs=(wide, wide),
-        compiler_params=pltpu.CompilerParams(vmem_limit_bytes=24 << 20),
+        out_specs=(tile, tile),
+        scratch_shapes=[pltpu.VMEM((rows, part), F32)],
+        compiler_params=pltpu.CompilerParams(vmem_limit_bytes=16 << 20),
         cost_estimate=pl.CostEstimate(
             flops=2 * fac.shape[0] * rows * cols, bytes_accessed=10 * rows * cols, transcendentals=0
         ),
@@ -364,15 +380,13 @@
 def on_device(global_params, local_params, momentum, init_factors, seeds, plan, round_index):
     shape = global_params.shape
     g, l, m = (x.reshape(shape[-2:]) for x in (global_params, local_params, momentum))
-    offset = plan[jnp.mod(round_index, plan.shape[0])]
-    island = lax.axis_index("island")
-    factor = init_factors[seeds[jnp.minimum(island, jnp.bitwise_xor(island, offset))], 0]
+    turns = jnp.arange(plan.shape[0], dtype=jnp.int32)
+    offset = jnp.sum(jnp.where(turns == lax.rem(round_index, plan.shape[0]), plan, 0))
     levels = lax.axis_size("island").bit_length() - 1
     shards = lax.axis_size("fsdp")
-    level_ids = jnp.arange(levels, dtype=jnp.int32)
-    which_bit = jnp.sum(jnp.where(jnp.left_shift(jnp.int32(1), level_ids) == offset, level_ids, 0))
+    which_bit = sum((offset > 1 << level).astype(jnp.int32) for level in range(levels))
     branches = [functools.partial(gossip, level, shards) for level in range(levels)]
-    warm, fac, bas = lax.switch(which_bit, branches, g, l, factor)
+    warm, fac, bas = lax.switch(which_bit, branches, seeds, g, l, init_factors[:, 0])
     params, velocity = outer_step(bas, fac, g, l, m)
     return params.reshape(shape), velocity.reshape(shape), warm[None, None]
 

time: 106 us -> 94.7 us (0.89)
  Pallas kernels: 91.5 us -> 86.1 us
  local copies, waits for them, and re-layouts: 7.43 us -> 4.03 us
  loops' own time: 1.95 us -> 0.02 us
    pallas_call x1, Pallas kernels: 71 us -> 65.9 us  [gossip(): pl.pallas_call(functools.partial(gossip_kernel, level, shards), out_shape...]
    dynamic_slice x2 -> x0, local copies, waits for them, and re-layouts: 2.49 us -> none  [the longest x1 1.24 us: on_device(): seeds[jnp.minimum(island, jnp.bitwise_xor(island, offset))]]
    another operation x1, loops' own time: 1.95 us -> 0.02 us  [on_device(): lax.switch(which_bit, branches, seeds, g, l, init_factors[:, 0])]
where the time goes in v1:
time: 94.7 us; the launch traced here: 94 us
  Pallas kernels  86.1 us (91%)
  local copies, waits for them, and re-layouts  4.03 us (4%)
  between operations  2.6 us (3%)
  other arithmetic  1.29 us (1%)
    pallas_call x1, Pallas kernels, gossip(): pl.pallas_call(functools.partial(gossip_kernel, level, shards), out_shape...  65.9 us
    pallas_call x1, Pallas kernels, outer_step(): pl.pallas_call(outer_kernel, grid=(cols // part,), out_shape=(jax.ShapeDt...  20.2 us
    unnamed x3, local copies, waits for them, and re-layouts  4.03 us

profile of v1, /device:TPU:0, one launch (start us, length us, event | category | flops | bytes accessed | tf_op | source)
XLA Modules:
  0.0 94.0 jit_solution(10090493283258360478)
XLA Ops:
  1.3 1.3 %fusion = s32[]{:T(128)} fusion(s32[8]{0:T(128)} %param.14, s32[]{:T(128)S(6)} %rem.18), kind=kLoop, calls=%fused_computation.1 | loop fusion | flops 23 | bytes 40 | tf_op jit(solution)/shard_map/reduce_sum | solution.py:384
  3.9 65.9 %conditional.1 = (bf16[16,8192]{1,0:T(8,128)(2,1)S(1)}, bf16[512,128]{1,0:T(8,128)(2,1)S(1)}, f32[1,1,4,8192]{3,2,1,0:T(4,128)S(1)}) conditional(s32[]{:T(128)} %clamp.3, (s32[4]{0:T(128)}, bf16[512,8192]{1,0:T(8,128)(2,1)}, bf16[512,8192]{1,0:T(8,128)(2,1)}, f32[4,4,8192]{2,1,0:T(4,128)}) %tuple.28, (s32[4]{0:T(128)}, bf16[512,8192]{1,0:T(8,128)(2,1)}, ...), branch_computations={%region_1.2_spmd, %region_2.3_spmd} | conditional | flops 603979776 | bytes 16777240 | solution.py:389
  3.9 65.9 %branch_0_fun.1 = (f32[4,8192]{1,0:T(4,128)S(1)}, bf16[16,8192]{1,0:T(8,128)(2,1)S(1)}, bf16[512,128]{1,0:T(8,128)(2,1)S(1)}) custom-call(s32[4]{0:T(128)} %get-tuple-element.23.seeds_ref, bf16[512,8192]{1,0:T(8,128)(2,1)} %get-tuple-element.24.g_hbm, bf16[512,8192]{1,0:T(8,128)(2,1)} %get-tuple-element.25.l_hbm, f32[4,4,8192]{2,1,0:T(4,128)} %get-tuple-element.26.init_ref), custom_call_target="tpu_custom_call" | custom-call | flops 603979776 | bytes 16777216 | tf_op jit(solution)/shard_map/cond/branch_0_fun/pallas_call | solution.py:305
  69.8 0.0 copy-start
  69.8 3.4 %copy-done = bf16[1,1,512,8192]{3,2,1,0:T(8,128)(2,1)S(1)} copy-done((bf16[1,1,512,8192]{3,2,1,0:T(8,128)(2,1)S(1)}, bf16[1,1,512,8192]{3,2,1,0:T(8,128)(2,1)}, u32[]{:S(2)}) %copy-start) | copy-done | bytes 8388632
  73.2 20.2 %shard_map.94 = (bf16[512,8192]{1,0:T(8,128)(2,1)}, bf16[512,8192]{1,0:T(8,128)(2,1)}) custom-call(bf16[512,128]{1,0:T(8,128)(2,1)S(1)} %get-tuple-element.45.bas_ref, bf16[16,8192]{1,0:T(8,128)(2,1)S(1)} %get-tuple-element.46.fac_ref, bf16[512,8192]{1,0:T(8,128)(2,1)} %bitcast.11, bf16[512,8192]{1,0:T(8,128)(2,1)} %bitcast.14, bf16[512,8192]{1,0:T(8,128)(2,1)S(1)} %bitcast.8), custom_call_target="tpu_custom_call" | custom-call | flops 134217728 | bytes 41943040 | tf_op jit(solution)/shard_map/pallas_call | solution.py:362
  93.3 0.7 copy.18
Async XLA Ops:
  69.8 3.4 %copy-start = (bf16[1,1,512,8192]{3,2,1,0:T(8,128)(2,1)S(1)}, bf16[1,1,512,8192]{3,2,1,0:T(8,128)(2,1)}, u32[]{:S(2)}) copy-start(bf16[1,1,512,8192]{3,2,1,0:T(8,128)(2,1)} %param.11) | copy-start | bytes 25165828

commit v2 on v1

--- a/solution.py
+++ b/solution.py
@@ -105,7 +105,7 @@
 
     part = g_buf.shape[2]
     parts = cols // part
-    tall = min(32, rows)
+    tall = min(64, rows)
 
     def load(i, slot):
         at = pl.ds(pl.multiple_of(i * part, part), part)
@@ -119,6 +119,18 @@
     seed = seeds_ref[jnp.minimum(island, island + (1 - 2 * side) * step)]
     acc[...] = jnp.zeros_like(acc)
 
+    def arrivals(ref, count, sem):
+        pltpu.make_async_remote_copy(
+            src_ref=ref.at[pl.ds(0, count)], dst_ref=ref.at[pl.ds(0, count)], send_sem=p_sem.at[0], recv_sem=sem,
+            device_id=(island + (1 - 2 * side) * step, shard), device_id_type=MESH,
+        ).wait_recv()
+
+    def departures(ref, count, sem):
+        pltpu.make_async_remote_copy(
+            src_ref=ref.at[pl.ds(0, count)], dst_ref=ref.at[pl.ds(0, count)], send_sem=sem, recv_sem=p_sem.at[1],
+            device_id=(island + (1 - 2 * side) * step, shard), device_id_type=MESH,
+        ).wait_send()
+
     def right(at, factor):
         parts = three_parts(factor)
         return dot(hi[:, at], parts, NT) + dot(lo[:, at], parts, NT)
@@ -135,12 +147,14 @@
         for copy in load(i, slot):
             copy.wait()
         at = pl.ds(pl.multiple_of(i * part, part), part)
+        factor = three_parts(init_ref[seed, :, at])
         for r in range(0, rows, tall):
             delta = g_buf[slot, r : r + tall].astype(F32) - l_buf[slot, r : r + tall].astype(F32)
             high = delta.astype(BF16)
+            low = (delta - high.astype(F32)).astype(BF16)
             hi[r : r + tall, at] = high
-            lo[r : r + tall, at] = (delta - high.astype(F32)).astype(BF16)
-        acc[:, 0 : 4 * rank] += right(at, init_ref[seed, :, at])
+            lo[r : r + tall, at] = low
+            acc[r : r + tall, 0 : 4 * rank] += dot(high, factor, NT) + dot(low, factor, NT)
 
     pl.semaphore_wait(barrier, members - 1)
 
@@ -169,16 +183,8 @@
             to = lax.rem(shard + k, shards)
             return pltpu.make_async_remote_copy(
                 src_ref=grams.at[turn, shard], dst_ref=grams.at[turn, shard],
-                send_sem=gram_send.at[turn, to], recv_sem=gram_recv.at[turn, shard],
+                send_sem=gram_send, recv_sem=gram_recv.at[turn],
                 device_id=(island, to), device_id_type=MESH,
-            )
-
-        def gram_arrival(k):
-            at = lax.rem(shard + k, shards)
-            return pltpu.make_async_remote_copy(
-                src_ref=grams.at[turn, at], dst_ref=grams.at[turn, at],
-                send_sem=gram_send.at[turn, at], recv_sem=gram_recv.at[turn, at],
-                device_id=(island, at), device_id_type=MESH,
             )
 
         @pl.loop(1, shards)
@@ -190,15 +196,8 @@
         def scatter(b):
             return pltpu.make_async_remote_copy(
                 src_ref=rs_out.at[b], dst_ref=rs_in.at[me],
-                send_sem=rs_send.at[b], recv_sem=rs_recv.at[me],
+                send_sem=rs_send, recv_sem=rs_recv,
                 device_id=device(b), device_id_type=MESH,
-            )
-
-        def scatter_arrival(k):
-            return pltpu.make_async_remote_copy(
-                src_ref=rs_out.at[k], dst_ref=rs_in.at[k],
-                send_sem=rs_send.at[k], recv_sem=rs_recv.at[k],
-                device_id=device(k), device_id_type=MESH,
             )
 
         @pl.loop(1, bundles + 1)
@@ -212,43 +211,44 @@
 
         rs_in[pl.ds(me, 1)] = rs_out[pl.ds(me, 1)]
 
-        @pl.loop(1, members)
-        def _(k):
-            scatter_arrival(after(members - k)).wait_recv()
-
+        arrivals(rs_in, members - 1, rs_recv)
         gathered[pl.ds(me, 1)] = jnp.sum(rs_in[...], axis=0, keepdims=True)
 
         def gather(b):
             return pltpu.make_async_remote_copy(
                 src_ref=gathered.at[me], dst_ref=gathered.at[me],
-                send_sem=ag_send.at[b], recv_sem=ag_recv.at[me],
+                send_sem=ag_send, recv_sem=ag_recv.at[mine],
                 device_id=device(b), device_id_type=MESH,
             )
 
-        def gather_arrival(k):
-            return pltpu.make_async_remote_copy(
-                src_ref=gathered.at[k], dst_ref=gathered.at[k],
-                send_sem=ag_send.at[k], recv_sem=ag_recv.at[k],
-                device_id=device(k), device_id_type=MESH,
-            )
+        def gathered_bundle(s):
+            k = lax.rem(mine + bundles - s, bundles)
+
+            @pl.when(s > 0)
+            def _():
+                arrivals(gathered, bundle, ag_recv.at[k])
+
+            if bundle > 1:
+
+                @pl.when(s == 0)
+                def _():
+                    arrivals(gathered, bundle - 1, ag_recv.at[k])
+
+            return k
 
         @pl.loop(0, bundles)
         def _(s):
             others(lax.rem(mine + s, bundles), lambda b: gather(b).start())
 
         def normaliser():
-            @pl.loop(1, shards)
-            def _(k):
-                gram_arrival(k).wait_recv()
-
+            arrivals(grams.at[turn], shards - 1, gram_recv.at[turn])
             return cholesky(jnp.sum(grams[turn], axis=0), rank)
 
         if turn < ITERS - 1:
 
             @pl.loop(0, bundles)
             def _(s):
-                k = lax.rem(mine + bundles - s, bundles)
-                others(k, lambda b: gather_arrival(b).wait_recv())
+                k = gathered_bundle(s)
                 factor = jnp.concatenate([gathered[k * bundle + j] for j in range(bundle)], axis=1)
                 total = right(columns(k), factor)
 
@@ -277,20 +277,13 @@
 
             @pl.loop(0, bundles)
             def _(s):
-                k = lax.rem(mine + bundles - s, bundles)
-                others(k, lambda b: gather_arrival(b).wait_recv())
+                k = gathered_bundle(s)
                 for j in range(bundle):
                     finish(k * bundle + j)
 
-        @pl.loop(1, members)
-        def _(k):
-            b = after(k)
-            scatter(b).wait_send()
-            gather(b).wait_send()
-
-        @pl.loop(1, shards)
-        def _(k):
-            gram_copy(k).wait_send()
+        departures(rs_out, members - 1, rs_send)
+        departures(gathered, members - 1, ag_send)
+        departures(grams.at[turn], shards - 1, gram_send)
 
 
 def gossip(level, shards, seeds, g, l, init):
@@ -298,6 +291,7 @@
     rank = init.shape[1]
     members = 2 * shards
     width = cols // members
+    bundles = members // 4 if members % 4 == 0 else members
     part = min(1024, cols)
     vmem = pl.BlockSpec(memory_space=pltpu.VMEM)
     hbm = pl.BlockSpec(memory_space=pl.ANY)
@@ -325,12 +319,12 @@
             pltpu.VMEM((ITERS, shards, rank, 128), F32),
             dma((2, 2)),
             dma((2,)),
-            dma((members,)),
-            dma((members,)),
-            dma((members,)),
-            dma((members,)),
-            dma((ITERS, shards)),
-            dma((ITERS, shards)),
+            dma,
+            dma,
+            dma,
+            dma((bundles,)),
+            dma,
+            dma((ITERS,)),
         ],
         compiler_params=pltpu.CompilerParams(
             collective_id=level + 1, has_side_effects=True, vmem_limit_bytes=30 << 20
@@ -357,7 +351,7 @@
 
 def outer_step(bas, fac, g, l, m):
     rows, cols = g.shape
-    part = min(512, cols)
+    part = min(1024, cols)
     tile = pl.BlockSpec((rows, part), lambda i: (0, i))
     return pl.pallas_call(
         outer_kernel,
@@ -370,7 +364,7 @@
         ],
         out_specs=(tile, tile),
         scratch_shapes=[pltpu.VMEM((rows, part), F32)],
-        compiler_params=pltpu.CompilerParams(vmem_limit_bytes=16 << 20),
+        compiler_params=pltpu.CompilerParams(vmem_limit_bytes=56 << 20),
         cost_estimate=pl.CostEstimate(
             flops=2 * fac.shape[0] * rows * cols, bytes_accessed=10 * rows * cols, transcendentals=0
         ),

time: 94.7 us -> 86.6 us (0.914)
  Pallas kernels: 86.1 us -> 81.8 us
  local copies, waits for them, and re-layouts: 4.03 us -> 0.66 us
    unnamed x3 -> x1, local copies, waits for them, and re-layouts: 4.03 us -> 0.66 us
    pallas_call x1, Pallas kernels: 65.9 us -> 63.6 us  [gossip(): pl.pallas_call(functools.partial(gossip_kernel, level, shards), out_shape...]
    pallas_call x1, Pallas kernels: 20.2 us -> 18.2 us  [outer_step(): pl.pallas_call(outer_kernel, grid=(cols // part,), out_shape=(jax.ShapeDt...]
where the time goes in v2:
time: 86.6 us; the launch traced here: 86.4 us
  Pallas kernels  81.8 us (94%)
  between operations  2.6 us (3%)
  other arithmetic  1.29 us (1%)
    pallas_call x1, Pallas kernels, gossip(): pl.pallas_call(functools.partial(gossip_kernel, level, shards), out_shape...  63.6 us
    pallas_call x1, Pallas kernels, outer_step(): pl.pallas_call(outer_kernel, grid=(cols // part,), out_shape=(jax.ShapeDt...  18.2 us

profile of v2, /device:TPU:0, one launch (start us, length us, event | category | flops | bytes accessed | tf_op | source)
XLA Modules:
  0.0 86.4 jit_solution(18294964889588114910)
XLA Ops:
  1.3 1.3 %fusion = s32[]{:T(128)} fusion(s32[8]{0:T(128)} %param.14, s32[]{:T(128)S(6)} %rem.18), kind=kLoop, calls=%fused_computation.1 | loop fusion | flops 23 | bytes 40 | tf_op jit(solution)/shard_map/reduce_sum | solution.py:378
  3.9 63.6 %conditional.1 = (bf16[16,8192]{1,0:T(8,128)(2,1)S(1)}, bf16[512,128]{1,0:T(8,128)(2,1)S(1)}, f32[1,1,4,8192]{3,2,1,0:T(4,128)S(1)}) conditional(s32[]{:T(128)} %clamp.3, (s32[4]{0:T(128)}, bf16[512,8192]{1,0:T(8,128)(2,1)}, bf16[512,8192]{1,0:T(8,128)(2,1)}, f32[4,4,8192]{2,1,0:T(4,128)}) %tuple.28, (s32[4]{0:T(128)}, bf16[512,8192]{1,0:T(8,128)(2,1)}, ...), branch_computations={%region_1.2_spmd, %region_2.3_spmd} | conditional | flops 603979776 | bytes 16777240 | solution.py:383
  3.9 63.6 %branch_0_fun.1 = (f32[4,8192]{1,0:T(4,128)S(1)}, bf16[16,8192]{1,0:T(8,128)(2,1)S(1)}, bf16[512,128]{1,0:T(8,128)(2,1)S(1)}) custom-call(s32[4]{0:T(128)} %get-tuple-element.23.seeds_ref, bf16[512,8192]{1,0:T(8,128)(2,1)} %get-tuple-element.24.g_hbm, bf16[512,8192]{1,0:T(8,128)(2,1)} %get-tuple-element.25.l_hbm, f32[4,4,8192]{2,1,0:T(4,128)} %get-tuple-element.26.init_ref), custom_call_target="tpu_custom_call" | custom-call | flops 603979776 | bytes 16777216 | tf_op jit(solution)/shard_map/cond/branch_0_fun/pallas_call | solution.py:299
  67.5 18.2 %shard_map.94 = (bf16[512,8192]{1,0:T(8,128)(2,1)}, bf16[512,8192]{1,0:T(8,128)(2,1)}) custom-call(bf16[512,128]{1,0:T(8,128)(2,1)S(1)} %get-tuple-element.45.bas_ref, bf16[16,8192]{1,0:T(8,128)(2,1)S(1)} %get-tuple-element.46.fac_ref, bf16[512,8192]{1,0:T(8,128)(2,1)} %bitcast.10, bf16[512,8192]{1,0:T(8,128)(2,1)} %bitcast.13, bf16[512,8192]{1,0:T(8,128)(2,1)} %bitcast.14), custom_call_target="tpu_custom_call" | custom-call | flops 134217728 | bytes 41943040 | tf_op jit(solution)/shard_map/pallas_call | solution.py:356
  85.7 0.7 copy.18

commit v3 on v2

--- a/solution.py
+++ b/solution.py
@@ -60,9 +60,9 @@
 
 
 def gossip_kernel(
-    level, shards, seeds_ref, g_hbm, l_hbm, init_ref, warm_ref, fac_ref, bas_ref,
-    hi, lo, g_buf, l_buf, acc, p_out, p_in, rs_out, rs_in, gathered, grams,
-    load_sem, p_sem, rs_send, rs_recv, ag_send, ag_recv, gram_send, gram_recv,
+    level, shards, seeds_ref, g_hbm, l_hbm, m_hbm, init_ref, warm_ref, fac_ref, bas_ref, hi, lo, g_ref, m_ref,
+    l_buf, acc, p_out, p_in, rs_out, rs_in, gathered, grams,
+    load_sem, m_sem, p_sem, rs_send, rs_recv, ag_send, ag_recv, gram_send, gram_recv,
 ):
     rank, cols = init_ref.shape[1:]
     rows = hi.shape[0]
@@ -103,14 +103,14 @@
     def _(k):
         pl.semaphore_signal(barrier, inc=1, device_id=device(after(k)), device_id_type=MESH)
 
-    part = g_buf.shape[2]
+    part = l_buf.shape[2]
     parts = cols // part
     tall = min(64, rows)
 
     def load(i, slot):
         at = pl.ds(pl.multiple_of(i * part, part), part)
         return (
-            pltpu.make_async_copy(g_hbm.at[:, at], g_buf.at[slot], load_sem.at[0, slot]),
+            pltpu.make_async_copy(g_hbm.at[:, at], g_ref.at[:, at], load_sem.at[0, slot]),
             pltpu.make_async_copy(l_hbm.at[:, at], l_buf.at[slot], load_sem.at[1, slot]),
         )
 
@@ -149,13 +149,15 @@
         at = pl.ds(pl.multiple_of(i * part, part), part)
         factor = three_parts(init_ref[seed, :, at])
         for r in range(0, rows, tall):
-            delta = g_buf[slot, r : r + tall].astype(F32) - l_buf[slot, r : r + tall].astype(F32)
+            delta = g_ref[r : r + tall, at].astype(F32) - l_buf[slot, r : r + tall].astype(F32)
             high = delta.astype(BF16)
             low = (delta - high.astype(F32)).astype(BF16)
             hi[r : r + tall, at] = high
             lo[r : r + tall, at] = low
             acc[r : r + tall, 0 : 4 * rank] += dot(high, factor, NT) + dot(low, factor, NT)
 
+    fill = pltpu.make_async_copy(m_hbm, m_ref, m_sem)
+    fill.start()
     pl.semaphore_wait(barrier, members - 1)
 
     factors = None
@@ -285,8 +287,10 @@
         departures(gathered, members - 1, ag_send)
         departures(grams.at[turn], shards - 1, gram_send)
 
-
-def gossip(level, shards, seeds, g, l, init):
+    fill.wait()
+
+
+def gossip(level, shards, seeds, g, l, m, init):
     rows, cols = g.shape
     rank = init.shape[1]
     members = 2 * shards
@@ -302,13 +306,11 @@
             jax.ShapeDtypeStruct((rank, cols), F32),
             jax.ShapeDtypeStruct((4 * rank, cols), BF16),
             jax.ShapeDtypeStruct((rows, 128), BF16),
-        ),
-        in_specs=[pl.BlockSpec(memory_space=pltpu.SMEM), hbm, hbm, vmem],
-        out_specs=(vmem, vmem, vmem),
+        )
+        + (pltpu.VMEM((rows, cols), BF16),) * 4,
+        in_specs=[pl.BlockSpec(memory_space=pltpu.SMEM), hbm, hbm, hbm, vmem],
+        out_specs=(vmem,) * 7,
         scratch_shapes=[
-            pltpu.VMEM((rows, cols), BF16),
-            pltpu.VMEM((rows, cols), BF16),
-            pltpu.VMEM((2, rows, part), BF16),
             pltpu.VMEM((2, rows, part), BF16),
             pltpu.VMEM((rows, 128), F32),
             pltpu.VMEM((rank, rows), F32),
@@ -318,6 +320,7 @@
             pltpu.VMEM((members, rank, width), F32),
             pltpu.VMEM((ITERS, shards, rank, 128), F32),
             dma((2, 2)),
+            dma,
             dma((2,)),
             dma,
             dma,
@@ -327,31 +330,31 @@
             dma((ITERS,)),
         ],
         compiler_params=pltpu.CompilerParams(
-            collective_id=level + 1, has_side_effects=True, vmem_limit_bytes=30 << 20
+            collective_id=level + 1, has_side_effects=True, vmem_limit_bytes=12 << 20
         ),
         cost_estimate=pl.CostEstimate(
             flops=12 * ITERS * rank * rows * cols, bytes_accessed=4 * rows * cols, transcendentals=0
         ),
-    )(seeds, g, l, init)
-
-
-def outer_kernel(bas_ref, fac_ref, g_ref, l_ref, m_ref, params_ref, momentum_ref, correction):
+    )(seeds, g, l, m, init)
+
+
+def outer_kernel(bas_ref, fac_ref, hi, lo, g_ref, m_ref, params_ref, momentum_ref, correction):
     depth = fac_ref.shape[0]
-    rows = g_ref.shape[0]
+    rows, part = params_ref.shape
     correction[...] = dot(bas_ref[:, 0:depth], fac_ref[...], NN)
     tall = min(32, rows)
+    columns = pl.ds(pl.multiple_of(pl.program_id(0) * part, part), part)
     for r in range(0, rows, tall):
         at = slice(r, r + tall)
-        start = g_ref[at].astype(F32)
-        gossiped = start - l_ref[at].astype(F32) - correction[at]
-        velocity = 0.9 * m_ref[at].astype(F32) + gossiped
-        params_ref[at] = (start - 0.7 * (gossiped + 0.9 * velocity)).astype(BF16)
+        gossiped = hi[at, columns].astype(F32) + (lo[at, columns].astype(F32) - correction[at])
+        velocity = 0.9 * m_ref[at, columns].astype(F32) + gossiped
+        params_ref[at] = (g_ref[at, columns].astype(F32) - 0.7 * (gossiped + 0.9 * velocity)).astype(BF16)
         momentum_ref[at] = velocity.astype(BF16)
 
 
-def outer_step(bas, fac, g, l, m):
-    rows, cols = g.shape
-    part = min(1024, cols)
+def outer_step(bas, fac, *whole):
+    rows, cols = whole[0].shape
+    part = min(512, cols)
     tile = pl.BlockSpec((rows, part), lambda i: (0, i))
     return pl.pallas_call(
         outer_kernel,
@@ -360,15 +363,15 @@
         in_specs=[
             pl.BlockSpec(bas.shape, lambda i: (0, 0)),
             pl.BlockSpec((fac.shape[0], part), lambda i: (0, i)),
-            tile, tile, tile,
-        ],
+        ]
+        + [pl.BlockSpec(memory_space=pltpu.VMEM)] * len(whole),
         out_specs=(tile, tile),
         scratch_shapes=[pltpu.VMEM((rows, part), F32)],
-        compiler_params=pltpu.CompilerParams(vmem_limit_bytes=56 << 20),
+        compiler_params=pltpu.CompilerParams(vmem_limit_bytes=12 << 20),
         cost_estimate=pl.CostEstimate(
-            flops=2 * fac.shape[0] * rows * cols, bytes_accessed=10 * rows * cols, transcendentals=0
+            flops=2 * fac.shape[0] * rows * cols, bytes_accessed=4 * rows * cols, transcendentals=0
         ),
-    )(bas, fac, g, l, m)
+    )(bas, fac, *(pltpu.with_memory_space_constraint(x, pltpu.VMEM) for x in whole))
 
 
 def on_device(global_params, local_params, momentum, init_factors, seeds, plan, round_index):
@@ -380,8 +383,8 @@
     shards = lax.axis_size("fsdp")
     which_bit = sum((offset > 1 << level).astype(jnp.int32) for level in range(levels))
     branches = [functools.partial(gossip, level, shards) for level in range(levels)]
-    warm, fac, bas = lax.switch(which_bit, branches, seeds, g, l, init_factors[:, 0])
-    params, velocity = outer_step(bas, fac, g, l, m)
+    warm, fac, bas, *whole = lax.switch(which_bit, branches, seeds, g, l, m, init_factors[:, 0])
+    params, velocity = outer_step(bas, fac, *whole)
     return params.reshape(shape), velocity.reshape(shape), warm[None, None]
 
 

time: 86.6 us -> 81.3 us (0.939)
  Pallas kernels: 81.8 us -> 76.5 us
    pallas_call x1, Pallas kernels: 18.2 us -> 12.8 us  [outer_step(): pl.pallas_call(outer_kernel, grid=(cols // part,), out_shape=(jax.ShapeDt...]
where the time goes in v3:
time: 81.3 us; the launch traced here: 81.1 us
  Pallas kernels  76.5 us (94%)
  between operations  2.6 us (3%)
  other arithmetic  1.29 us (2%)
    pallas_call x1, Pallas kernels, gossip(): pl.pallas_call(functools.partial(gossip_kernel, level, shards), out_shape...  63.6 us
    pallas_call x1, Pallas kernels, outer_step(): pl.pallas_call(outer_kernel, grid=(cols // part,), out_shape=(jax.ShapeDt...  12.8 us

profile of v3, /device:TPU:0, one launch (start us, length us, event | category | flops | bytes accessed | tf_op | source)
XLA Modules:
  0.0 81.1 jit_solution(8383021612359925807)
XLA Ops:
  1.3 1.3 %fusion = s32[]{:T(128)} fusion(s32[8]{0:T(128)} %param.14, s32[]{:T(128)S(6)} %rem.18), kind=kLoop, calls=%fused_computation.1 | loop fusion | flops 23 | bytes 40 | tf_op jit(solution)/shard_map/reduce_sum | solution.py:381
  3.9 63.7 %conditional.1 = ((f32[4,8192]{1,0:T(4,128)S(1)}, bf16[16,8192]{1,0:T(8,128)(2,1)S(1)}, bf16[512,128]{1,0:T(8,128)(2,1)S(1)}, bf16[512,8192]{1,0:T(8,128)(2,1)S(...) conditional(s32[]{:T(128)} %clamp.3, (s32[4]{0:T(128)}, ...), branch_computations={%region_1.2_spmd, %region_2.3_spmd} | conditional | flops 603979776 | bytes 16777224 | solution.py:386
  3.9 63.6 %branch_1_fun.1 = (f32[4,8192]{1,0:T(4,128)S(1)}, bf16[16,8192]{1,0:T(8,128)(2,1)S(1)}, bf16[512,128]{1,0:T(8,128)(2,1)S(1)}, bf16[512,8192]{1,0:T(8,128)(2,1)S(...) custom-call(s32[4]{0:T(128)} %get-tuple-element.48.seeds_ref, ...), custom_call_target="tpu_custom_call" | custom-call | flops 603979776 | bytes 16777216 | tf_op jit(solution)/shard_map/cond/branch_1_fun/pallas_call | solution.py:303
  67.6 12.8 %shard_map.94 = (bf16[512,8192]{1,0:T(8,128)(2,1)}, bf16[512,8192]{1,0:T(8,128)(2,1)}) custom-call(bf16[512,128]{1,0:T(8,128)(2,1)S(1)} %get-tuple-element.95.bas_ref, bf16[16,8192]{1,0:T(8,128)(2,1)S(1)} %get-tuple-element.96.fac_ref, bf16[512,8192]{1,0:T(8,128)(2,1)S(1)} %get-tuple-element.94.hi, bf16[512,8192]{1,0:T(8,128)(2,1)S(1)} %get-tuple-element.93.lo, ...), custom_call_target="tpu_custom_call" | custom-call | flops 134217728 | bytes 16777216 | tf_op jit(solution)/shard_map/pallas_call | solution.py:359
  80.4 0.7 copy.26

commit v4 on v3

--- a/solution.py
+++ b/solution.py
@@ -174,25 +174,6 @@
         swap.wait()
         left = product - p_in[...]
 
-        lane = lax.broadcasted_iota(jnp.int32, (rank, 128), 1)
-        gram = jnp.zeros((rank, 128), F32)
-        for j in range(rank):
-            column = jnp.sum(left * left[j : j + 1], axis=1, keepdims=True)
-            gram = jnp.where(lane == j, column, gram)
-        grams[turn, pl.ds(shard, 1)] = gram[None]
-
-        def gram_copy(k):
-            to = lax.rem(shard + k, shards)
-            return pltpu.make_async_remote_copy(
-                src_ref=grams.at[turn, shard], dst_ref=grams.at[turn, shard],
-                send_sem=gram_send, recv_sem=gram_recv.at[turn],
-                device_id=(island, to), device_id_type=MESH,
-            )
-
-        @pl.loop(1, shards)
-        def _(k):
-            gram_copy(k).start()
-
         left_parts = three_parts(left)
 
         def scatter(b):
@@ -213,6 +194,25 @@
 
         rs_in[pl.ds(me, 1)] = rs_out[pl.ds(me, 1)]
 
+        lane = lax.broadcasted_iota(jnp.int32, (rank, 128), 1)
+        gram = jnp.zeros((rank, 128), F32)
+        for j in range(rank):
+            column = jnp.sum(left * left[j : j + 1], axis=1, keepdims=True)
+            gram = jnp.where(lane == j, column, gram)
+        grams[turn, pl.ds(shard, 1)] = gram[None]
+
+        def gram_copy(k):
+            to = lax.rem(shard + k, shards)
+            return pltpu.make_async_remote_copy(
+                src_ref=grams.at[turn, shard], dst_ref=grams.at[turn, shard],
+                send_sem=gram_send, recv_sem=gram_recv.at[turn],
+                device_id=(island, to), device_id_type=MESH,
+            )
+
+        @pl.loop(1, shards)
+        def _(k):
+            gram_copy(k).start()
+
         arrivals(rs_in, members - 1, rs_recv)
         gathered[pl.ds(me, 1)] = jnp.sum(rs_in[...], axis=0, keepdims=True)
 
@@ -246,6 +246,7 @@
             arrivals(grams.at[turn], shards - 1, gram_recv.at[turn])
             return cholesky(jnp.sum(grams[turn], axis=0), rank)
 
+        factors = normaliser()
         if turn < ITERS - 1:
 
             @pl.loop(0, bundles)
@@ -262,9 +263,7 @@
                 def _():
                     acc[:, 0 : 4 * rank] += total
 
-            factors = normaliser()
         else:
-            factors = normaliser()
             basis = 0.5 * solved(factors, left)
             high = rounded(basis)
             stack = jnp.concatenate([high, high, basis - high, jnp.zeros_like(basis)], axis=0)
@@ -338,15 +337,16 @@
     )(seeds, g, l, m, init)
 
 
-def outer_kernel(bas_ref, fac_ref, hi, lo, g_ref, m_ref, params_ref, momentum_ref, correction):
+def outer_kernel(bas_ref, fac_ref, hi, lo, g_ref, m_ref, params_ref, momentum_ref):
     depth = fac_ref.shape[0]
     rows, part = params_ref.shape
-    correction[...] = dot(bas_ref[:, 0:depth], fac_ref[...], NN)
-    tall = min(32, rows)
+    factor = fac_ref[...]
+    tall = min(64, rows)
     columns = pl.ds(pl.multiple_of(pl.program_id(0) * part, part), part)
     for r in range(0, rows, tall):
         at = slice(r, r + tall)
-        gossiped = hi[at, columns].astype(F32) + (lo[at, columns].astype(F32) - correction[at])
+        correction = dot(bas_ref[at, 0:depth], factor, NN)
+        gossiped = hi[at, columns].astype(F32) + (lo[at, columns].astype(F32) - correction)
         velocity = 0.9 * m_ref[at, columns].astype(F32) + gossiped
         params_ref[at] = (g_ref[at, columns].astype(F32) - 0.7 * (gossiped + 0.9 * velocity)).astype(BF16)
         momentum_ref[at] = velocity.astype(BF16)
@@ -366,7 +366,6 @@
         ]
         + [pl.BlockSpec(memory_space=pltpu.VMEM)] * len(whole),
         out_specs=(tile, tile),
-        scratch_shapes=[pltpu.VMEM((rows, part), F32)],
         compiler_params=pltpu.CompilerParams(vmem_limit_bytes=12 << 20),
         cost_estimate=pl.CostEstimate(
             flops=2 * fac.shape[0] * rows * cols, bytes_accessed=4 * rows * cols, transcendentals=0

time: 81.3 us -> 80.4 us (0.989)
  Pallas kernels: 76.5 us -> 75.5 us
    pallas_call x1, Pallas kernels: 63.6 us -> 62.8 us  [gossip(): pl.pallas_call(functools.partial(gossip_kernel, level, shards), out_shape...]
where the time goes in v4:
time: 80.4 us; the launch traced here: 80.1 us
  Pallas kernels  75.5 us (94%)
  between operations  2.6 us (3%)
  other arithmetic  1.29 us (2%)
    pallas_call x1, Pallas kernels, gossip(): pl.pallas_call(functools.partial(gossip_kernel, level, shards), out_shape...  62.8 us
    pallas_call x1, Pallas kernels, outer_step(): pl.pallas_call(outer_kernel, grid=(cols // part,), out_shape=(jax.ShapeDt...  12.8 us

profile of v4, /device:TPU:0, one launch (start us, length us, event | category | flops | bytes accessed | tf_op | source)
XLA Modules:
  0.0 80.1 jit_solution(9641634476192370786)
XLA Ops:
  1.3 1.3 %fusion = s32[]{:T(128)} fusion(s32[8]{0:T(128)} %param.14, s32[]{:T(128)S(6)} %rem.18), kind=kLoop, calls=%fused_computation.1 | loop fusion | flops 23 | bytes 40 | tf_op jit(solution)/shard_map/reduce_sum | solution.py:380
  3.9 62.8 %conditional.1 = ((f32[4,8192]{1,0:T(4,128)S(1)}, bf16[16,8192]{1,0:T(8,128)(2,1)S(1)}, bf16[512,128]{1,0:T(8,128)(2,1)S(1)}, bf16[512,8192]{1,0:T(8,128)(2,1)S(...) conditional(s32[]{:T(128)} %clamp.3, (s32[4]{0:T(128)}, ...), branch_computations={%region_1.2_spmd, %region_2.3_spmd} | conditional | flops 603979776 | bytes 16777224 | solution.py:385
  3.9 62.8 %branch_1_fun.1 = (f32[4,8192]{1,0:T(4,128)S(1)}, bf16[16,8192]{1,0:T(8,128)(2,1)S(1)}, bf16[512,128]{1,0:T(8,128)(2,1)S(1)}, bf16[512,8192]{1,0:T(8,128)(2,1)S(...) custom-call(s32[4]{0:T(128)} %get-tuple-element.48.seeds_ref, ...), custom_call_target="tpu_custom_call" | custom-call | flops 603979776 | bytes 16777216 | tf_op jit(solution)/shard_map/cond/branch_1_fun/pallas_call | solution.py:302
  66.7 12.8 %shard_map.94 = (bf16[512,8192]{1,0:T(8,128)(2,1)}, bf16[512,8192]{1,0:T(8,128)(2,1)}) custom-call(bf16[512,128]{1,0:T(8,128)(2,1)S(1)} %get-tuple-element.95.bas_ref, bf16[16,8192]{1,0:T(8,128)(2,1)S(1)} %get-tuple-element.96.fac_ref, bf16[512,8192]{1,0:T(8,128)(2,1)S(1)} %get-tuple-element.94.hi, bf16[512,8192]{1,0:T(8,128)(2,1)S(1)} %get-tuple-element.93.lo, ...), custom_call_target="tpu_custom_call" | custom-call | flops 134217728 | bytes 16777216 | tf_op jit(solution)/shard_map/pallas_call | solution.py:359
  79.5 0.7 copy.26
